TPU v7x, 32 devices: a whole 2x2x4 slice. The times are simulated.
32 devices in a mesh: groups: 2 (over x), ctx: 16 (over z, y, core).
Axes of the slice: x: 2, y: 2, z: 4, core: 2. Of those that a mesh axis runs over, the one named last changes fastest.
Arguments:
- pool_keys: bfloat16 [4096, 1024], P(('groups', 'ctx')), parts along dimension 0, may hold values from -6 to 6
- pool_values: bfloat16 [4096, 1024], P(('groups', 'ctx')), parts along dimension 0, may hold values from -6 to 6
- key_scales: float32 [256, 8], P(('groups', 'ctx')), parts along dimension 0, may hold values from 0.25 to 2
- value_scales: float32 [256, 8], P(('groups', 'ctx')), parts along dimension 0, may hold values from 0.25 to 2
- page_source: int32 [256], P('groups'), parts along dimension 0, may hold values from 0 to 127, as said below
- page_lengths: int32 [256], P('groups'), parts along dimension 0, may hold values from 10 to 16
- page_offsets: int32 [256], P('groups'), parts along dimension 0, may hold values from 0 to 1899, as said below
- query_positions: int32 [256], P('groups'), parts along dimension 0, may hold values from 0 to 2047
- queries: bfloat16 [256, 16384], P('groups', 'ctx'), parts along dimension 0, may hold values from -64 to 64
- out_weight: bfloat16 [16384, 16384], P('ctx'), may hold values from -0.046875 to 0.046875
Outputs:
- new_keys: bfloat16 [4096, 1024], P(('groups', 'ctx')), parts along dimension 0
- new_values: bfloat16 [4096, 1024], P(('groups', 'ctx')), parts along dimension 0
- output: bfloat16 [256, 16384], P('groups', 'ctx'), parts along dimension 0
There are 2 independent parts, one for each index of `groups`. A program takes and returns all parts, laid end to end along the dimension named above; an argument that names none is the same for every part. Nothing has to cross between parts.
Inputs may be any that keep to these rules, and one draw needn't show every extreme that they name: `page_source`: a permutation of the pool pages; the 8 pages of one device's part of the new context come from 8 different devices, and the 8 pool pages of one device go to 8 different devices. page_offsets[0] is 0, and page_offsets[c + 1] - page_offsets[c] is page_lengths[c] plus 0 to 4.
All inputs are finite; a program needn't handle non-finite values.
Results may differ from a plain program's by a relative error of at most 0.012.
The roundings to bfloat16 on the way count: a program that leaves them out, or rounds other values in their place, can miss the bound.
Values may be sent and summed in bfloat16 or wider, within the bound.
A program may use at most 128 MiB of HBM per device.

v0:
```python
import math

import jax
import jax.numpy as jnp
from jax import lax
from jax.sharding import PartitionSpec as P

H = 128
KV = 8
HD = 128
PAGE = 16


rope_theta = 500000.0
scale_factor = 8.0
low_factor = 1.0
high_factor = 4.0
old_context = 8192.0
masked_score = -1e30


def inverse_freq():
    exponent = jnp.arange(0, HD, 2).astype(jnp.float32) / HD
    base_freq = 1.0 / rope_theta**exponent
    wavelength = 2.0 * math.pi / base_freq
    smooth = (old_context / wavelength - low_factor) / (high_factor - low_factor)
    blended = (1.0 - smooth) * base_freq / scale_factor + smooth * base_freq
    short_wave = wavelength < old_context / high_factor
    longer = wavelength > old_context / low_factor
    return jnp.where(short_wave, base_freq, jnp.where(longer, base_freq / scale_factor, blended))


def rotate(values, positions):
    angle = positions.astype(jnp.float32)[:, None] * inverse_freq()[None, :]
    cosine = jnp.cos(angle)[:, None, :]
    sine_part = jnp.sin(angle)[:, None, :]
    half_size = values.shape[-1] // 2
    first_half = values[..., :half_size]
    second = values[..., half_size:]
    return jnp.concatenate(
        [first_half * cosine - second * sine_part, second * cosine + first_half * sine_part],
        axis=-1,
    )


def body(
    pool_keys,
    pool_values,
    key_scales,
    value_scales,
    page_source,
    page_lengths,
    page_offsets,
    query_positions,
    queries,
    out_weight,
):
    devices = lax.axis_size("ctx")
    here_index = lax.axis_index("ctx")
    slot_count = key_scales.shape[0]
    page_count = page_source.shape[0]
    query_count = queries.shape[0]
    local_heads = queries.shape[1] // HD
    per_group = H // KV
    in_page = jnp.arange(PAGE, dtype=jnp.int32)
    inverse = (
        jnp.zeros((page_count,), jnp.int32)
        .at[page_source]
        .set(jnp.arange(page_count, dtype=jnp.int32))
    )
    held_pages = lax.dynamic_slice_in_dim(inverse, here_index * slot_count, slot_count)
    held_live = in_page[None, :] < page_lengths[held_pages][:, None]
    live_float = held_live.reshape(-1).astype(jnp.float32)[:, None, None]
    scaled_keys = (
        pool_keys.reshape(slot_count, PAGE, KV, HD).astype(jnp.float32)
        * key_scales[:, None, :, None]
    )
    scaled_values = (
        pool_values.reshape(slot_count, PAGE, KV, HD).astype(jnp.float32)
        * value_scales[:, None, :, None]
    )
    turned = rotate(
        scaled_keys.reshape(slot_count * PAGE, KV, HD), jnp.repeat(page_offsets[held_pages], PAGE)
    )
    slot_keys = (turned * live_float).astype(jnp.bfloat16).reshape(slot_count, PAGE * KV * HD)
    slot_values = (
        (scaled_values.reshape(slot_count * PAGE, KV, HD) * live_float)
        .astype(jnp.bfloat16)
        .reshape(slot_count, PAGE * KV * HD)
    )
    owner_device = held_pages // slot_count
    routing = (owner_device[None, :] == jnp.arange(devices, dtype=jnp.int32)[:, None]).astype(
        jnp.bfloat16
    )
    outgoing_keys = jnp.dot(routing, slot_keys, preferred_element_type=jnp.float32).astype(
        jnp.bfloat16
    )
    outgoing_values = jnp.dot(routing, slot_values, preferred_element_type=jnp.float32).astype(
        jnp.bfloat16
    )
    arrived_keys, arrived_values = (
        lax.all_to_all(outgoing_keys, "ctx", split_axis=0, concat_axis=0, tiled=True),
        lax.all_to_all(outgoing_values, "ctx", split_axis=0, concat_axis=0, tiled=True),
    )
    assembled_pages = here_index * slot_count + jnp.arange(slot_count, dtype=jnp.int32)
    sender = page_source[assembled_pages] // slot_count
    new_keys = arrived_keys[sender].reshape(slot_count * PAGE, KV * HD)
    new_values = arrived_values[sender].reshape(slot_count * PAGE, KV * HD)
    local_keys = slot_keys.reshape(slot_count * PAGE, KV * HD)
    local_values = slot_values.reshape(slot_count * PAGE, KV * HD)
    local_tokens = local_keys.shape[0]
    turned_q = rotate(
        queries.astype(jnp.float32).reshape(query_count, local_heads, HD), query_positions
    )
    own_queries = turned_q.astype(jnp.bfloat16).transpose(1, 0, 2)
    target = jnp.arange(devices, dtype=jnp.int32) * local_heads // per_group
    keys_by_head = local_keys.reshape(local_tokens, KV, HD).transpose(1, 0, 2)
    values_by_head = local_values.reshape(local_tokens, KV, HD).transpose(1, 0, 2)
    head_keys, head_values = (
        lax.all_to_all(keys_by_head[target], "ctx", split_axis=0, concat_axis=0, tiled=True),
        lax.all_to_all(values_by_head[target], "ctx", split_axis=0, concat_axis=0, tiled=True),
    )
    key_positions = (page_offsets[inverse][:, None] + in_page[None, :]).reshape(-1)
    key_live = (in_page[None, :] < page_lengths[inverse][:, None]).reshape(-1)
    key_positions, key_live = (key_positions, key_live)
    allowed = (key_positions[None, :] <= query_positions[:, None]) & key_live[None, :]
    span_devices = max(1, min(devices, 4096 // local_tokens))
    while span_devices > 1 and devices % span_devices:
        span_devices -= 1
    block_count = devices // span_devices
    key_blocks = head_keys.reshape(block_count, span_devices * local_tokens, HD)
    value_blocks = head_values.reshape(block_count, span_devices * local_tokens, HD)
    allowed_blocks = allowed.reshape(
        query_count, block_count, span_devices * local_tokens
    ).transpose(1, 0, 2)

    def block_scores(key_block, allow_block):
        scores = jnp.einsum(
            "hqd,kd->hqk", own_queries, key_block, preferred_element_type=jnp.float32
        ) * HD ** (-0.5)
        return jnp.where(allow_block[None], scores, masked_score)

    block_max = lax.map(
        lambda operands: jnp.max(block_scores(operands[0], operands[1]), axis=-1),
        (key_blocks, allowed_blocks),
    )
    row_max = jnp.max(block_max, axis=0)

    def weigh_block(operands):
        key_block, value_block, allow_block = operands
        weights = jnp.exp(block_scores(key_block, allow_block) - row_max[..., None])
        denominator = jnp.sum(weights, axis=-1)
        summed = jnp.einsum(
            "hqk,kd->hqd",
            weights.astype(jnp.bfloat16),
            value_block,
            preferred_element_type=jnp.float32,
        )
        return (summed, denominator)

    summed, denominator = lax.map(weigh_block, (key_blocks, value_blocks, allowed_blocks))
    summed = jnp.sum(summed, axis=0)
    denominator = jnp.sum(denominator, axis=0)
    attended = (summed / denominator[..., None]).astype(jnp.bfloat16)
    mixed = attended.transpose(1, 0, 2).reshape(query_count, local_heads * HD)
    reduced = lax.psum_scatter(
        lax.dot_general(
            out_weight, mixed, (((0,), (1,)), ((), ())), preferred_element_type=jnp.float32
        ),
        "ctx",
        scatter_dimension=0,
        tiled=True,
    )
    output = reduced.T.astype(jnp.bfloat16)
    return (new_keys, new_values, output)


def solution(mesh):
    in_specs = (
        P(("groups", "ctx"), None),
        P(("groups", "ctx"), None),
        P(("groups", "ctx"), None),
        P(("groups", "ctx"), None),
        P("groups"),
        P("groups"),
        P("groups"),
        P("groups"),
        P("groups", "ctx"),
        P("ctx", None),
    )
    out_specs = (P(("groups", "ctx"), None), P(("groups", "ctx"), None), P("groups", "ctx"))
    return jax.shard_map(body, mesh=mesh, in_specs=in_specs, out_specs=out_specs, check_vma=False)
```

profile of v0, /device:TPU:0, one launch (start us, length us, event | category | flops | bytes accessed | tf_op | source)
XLA Modules:
  0.0 205.9 jit_solution(7012284958098721424)
XLA Ops:
  7.2 0.7 compare_select_fusion.4
  7.9 0.7 convert_element_type.102
  8.6 1.0 scatter_custom_fusion
  9.7 0.6 gather_fusion.1
  10.3 1.3 gather_fusion
  12.0 0.8 copy.50
  12.7 0.8 copy.57
  13.8 1.1 copy.55
  14.9 1.1 copy.49
  16.7 0.5 multiply_cosine_fusion
  17.2 0.3 multiply_subtract_fusion
  17.5 0.4 fusion.17
  17.9 1.4 gather_fusion.7
  19.3 7.4 %all-to-all-start.2 = ((bf16[16,128,128]{2,1,0:T(8,128)(2,1)}), bf16[16,128,128]{2,1,0:T(8,128)(2,1)S(1)}, u32[]{:S(2)}, u32[]{:S(2)}) async-start(bf16[16,128,128]{2,1,0:T(8,128)(2,1)} %gather_fusion.7), calls=%async_computation.2 | async-start | bytes 1048576 | tf_op jit(solution)/shard_map/all_to_all | solution.py:120
  26.7 1.2 gather_fusion.6
  28.0 1.2 gather_fusion.5
  30.2 1.4 gather_fusion.8
  32.1 9.1 %all-to-all-done.2 = bf16[16,128,128]{2,1,0:T(8,128)(2,1)S(1)} async-done(((bf16[16,128,128]{2,1,0:T(8,128)(2,1)}), bf16[16,128,128]{2,1,0:T(8,128)(2,1)S(1)}, u32[]{:S(2)}, u32[]{:S(2)}) %all-to-all-start.2) | async-done | bytes 524320 | tf_op jit(solution)/shard_map/all_to_all | solution.py:120
  41.2 4.1 %all-to-all-start.3 = ((bf16[16,128,128]{2,1,0:T(8,128)(2,1)}), bf16[16,128,128]{2,1,0:T(8,128)(2,1)S(1)}, u32[]{:S(2)}, u32[]{:S(2)}) async-start(bf16[16,128,128]{2,1,0:T(8,128)(2,1)} %gather_fusion.8), calls=%async_computation.3 | async-start | bytes 1048576 | tf_op jit(solution)/shard_map/all_to_all | solution.py:121
  45.5 1.7 fusion.2
  47.2 3.2 %copy-done.4 = f32[8,128,2048]{2,1,0:T(8,128)} copy-done((f32[8,128,2048]{2,1,0:T(8,128)}, f32[8,128,2048]{2,1,0:T(8,128)S(1)}, u32[]{:S(2)}) %copy-start.4) | copy-done | bytes 8388632
  50.5 2.2 %fusion.3 = f32[8,128]{1,0:T(8,128)S(1)} fusion(f32[8,128,2048]{2,1,0:T(8,128)S(1)} %get-tuple-element.60, f32[8,128]{1,0:T(8,128)S(1)} %get-tuple-element.59, pred[128,2048]{1,0:T(8,128)(4,1)S(1)} %compare_and_fusion), kind=kLoop, calls=%fused_computation.18 | loop fusion | flops 8387584 | bytes 8658944 | tf_op jit(solution)/shard_map/while/body/eval_jaxpr/reduce_sum | solution.py:152
  52.7 7.0 %all-to-all-done.3 = bf16[16,128,128]{2,1,0:T(8,128)(2,1)S(1)} async-done(((bf16[16,128,128]{2,1,0:T(8,128)(2,1)}), bf16[16,128,128]{2,1,0:T(8,128)(2,1)S(1)}, u32[]{:S(2)}, u32[]{:S(2)}) %all-to-all-start.3) | async-done | bytes 524320 | tf_op jit(solution)/shard_map/all_to_all | solution.py:121
  59.7 5.5 %fusion.14 = bf16[128,8,128]{0,2,1:T(8,128)(2,1)S(1)} fusion(bf16[2048,128,1]{1,0,2:T(8,128)(2,1)S(1)} %bitcast.74, f32[8,128,2048]{2,1,0:T(8,128)} %copy-done.4, f32[8,128]{1,0:T(8,128)S(1)} %get-tuple-element.59, pred[128,2048]{1,0:T(8,128)(4,1)S(1)} %compare_and_fusion, f32[128,8]{0,1:T(8,128)S(1)} %bitcast.76), kind=kOutput, calls=%fused_computation.25 | convolution fusion | flops 545521664 | bytes 9445376 | tf_op jit(solution)/shard_map/while/body/eval_jaxpr/hqk,kd->hqd/dot_general | solution.py:153
  65.2 18.6 %convolution_bitcast_fusion = f32[16384,128]{0,1:T(8,128)} fusion(bf16[128,1024]{0,1:T(8,128)(2,1)S(1)} %bitcast.75, bf16[1024,16384]{1,0:T(8,128)(2,1)} %param.19), kind=kOutput, calls=%fused_computation.10 | convolution fusion | flops 4294967296 | bytes 42205184 | tf_op jit(solution)/shard_map/dot_general | solution.py:167
  84.8 0.3 fusion.1
  85.1 0.5 broadcast.458
  85.6 1.0 reduce.1
  86.6 1.2 reshape.473
  87.8 4.1 %all-to-all-start.1 = ((bf16[16,2,8192]{2,1,0:T(2,128)(2,1)}), bf16[16,2,8192]{2,1,0:T(2,128)(2,1)S(1)}, u32[]{:S(2)}, u32[]{:S(2)}) async-start(bf16[16,2,8192]{2,1,0:T(2,128)(2,1)} %reshape.473), calls=%async_computation.1 | async-start | bytes 1048576 | tf_op jit(solution)/shard_map/all_to_all | solution.py:103
  91.9 0.3 copy.52
  92.4 0.3 fusion
  92.7 1.0 reduce
  93.7 1.2 reshape.471
  94.9 11.5 %all-to-all-done.1 = bf16[16,2,8192]{2,1,0:T(2,128)(2,1)S(1)} async-done(((bf16[16,2,8192]{2,1,0:T(2,128)(2,1)}), bf16[16,2,8192]{2,1,0:T(2,128)(2,1)S(1)}, u32[]{:S(2)}, u32[]{:S(2)}) %all-to-all-start.1) | async-done | bytes 524320 | tf_op jit(solution)/shard_map/all_to_all | solution.py:103
  106.4 4.1 %all-to-all-start = ((bf16[16,2,8192]{2,1,0:T(2,128)(2,1)}), bf16[16,2,8192]{2,1,0:T(2,128)(2,1)S(1)}, u32[]{:S(2)}, u32[]{:S(2)}) async-start(bf16[16,2,8192]{2,1,0:T(2,128)(2,1)} %reshape.471), calls=%async_computation | async-start | bytes 1048576 | tf_op jit(solution)/shard_map/all_to_all | solution.py:102
  110.5 0.6 gather_fusion.2
  111.2 0.5 reshape.474
  111.8 0.6 copy.73
  112.3 0.7 gather_fusion.4
  113.1 0.8 reshape.372
  113.9 16.3 %all-to-all-done = bf16[16,2,8192]{2,1,0:T(2,128)(2,1)S(1)} async-done(((bf16[16,2,8192]{2,1,0:T(2,128)(2,1)}), bf16[16,2,8192]{2,1,0:T(2,128)(2,1)S(1)}, u32[]{:S(2)}, u32[]{:S(2)}) %all-to-all-start) | async-done | bytes 524320 | tf_op jit(solution)/shard_map/all_to_all | solution.py:102
  130.2 0.5 reshape.472
  130.8 0.6 copy.74
  131.3 0.7 gather_fusion.3
  132.1 0.8 reshape.371
  132.9 64.4 %reduce-scatter.2.cloned.1.call-done = f32[1024,128]{0,1:T(8,128)} async-done(((f32[16384,128]{0,1:T(8,128)}), f32[1024,128]{0,1:T(8,128)}) %reduce-scatter.2.cloned.1.call-update) | async-done | bytes 524304 | tf_op jit(solution)/shard_map/reduce_scatter | solution.py:166
  197.3 1.8 convert_bitcast_fusion
  (58 shorter events, 4.0 us)
Async XLA Ops:
  7.2 2.5 %copy-start = (s32[128]{0:T(128)S(1)}, s32[128]{0:T(128)}, u32[]{:S(2)}) copy-start(s32[128]{0:T(128)} %param.15) | copy-start | bytes 1540
  7.2 20.8 %copy-start.2 = (s32[128]{0:T(128)S(1)}, s32[128]{0:T(128)}, u32[]{:S(2)}) copy-start(s32[128]{0:T(128)} %param.16) | copy-start | bytes 1540
  7.2 22.4 %copy-start.5 = (bf16[128,1024]{1,0:T(8,128)(2,1)S(1)}, bf16[128,1024]{1,0:T(8,128)(2,1)}, u32[]{:S(2)}) copy-start(bf16[128,1024]{1,0:T(8,128)(2,1)} %param.18) | copy-start | bytes 786436
  16.3 15.6 %copy-start.6 = (s32[128]{0:T(128)S(1)}, s32[128]{0:T(128)}, u32[]{:S(2)}) copy-start(s32[128]{0:T(128)} %param.17) | copy-start | bytes 1540
  19.3 21.9 %all-to-all-start.2 = ((bf16[16,128,128]{2,1,0:T(8,128)(2,1)}), bf16[16,128,128]{2,1,0:T(8,128)(2,1)S(1)}, u32[]{:S(2)}, u32[]{:S(2)}) async-start(bf16[16,128,128]{2,1,0:T(8,128)(2,1)} %gather_fusion.7), calls=%async_computation.2 | async-start | bytes 1048576 | tf_op jit(solution)/shard_map/all_to_all | solution.py:120
  41.2 18.6 %all-to-all-start.3 = ((bf16[16,128,128]{2,1,0:T(8,128)(2,1)}), bf16[16,128,128]{2,1,0:T(8,128)(2,1)S(1)}, u32[]{:S(2)}, u32[]{:S(2)}) async-start(bf16[16,128,128]{2,1,0:T(8,128)(2,1)} %gather_fusion.8), calls=%async_computation.3 | async-start | bytes 1048576 | tf_op jit(solution)/shard_map/all_to_all | solution.py:121
  45.3 152.0 %reduce-scatter.2.cloned.1.call-start = ((), (), s32[]{:S(2)}) async-start(), calls=%async_computation.5 | async-start | bytes 8912896 | tf_op jit(solution)/shard_map/reduce_scatter | solution.py:166
  47.2 3.2 %copy-start.4 = (f32[8,128,2048]{2,1,0:T(8,128)}, f32[8,128,2048]{2,1,0:T(8,128)S(1)}, u32[]{:S(2)}) copy-start(f32[8,128,2048]{2,1,0:T(8,128)S(1)} %get-tuple-element.60) | copy-start | bytes 25165828
  83.9 26.6 %copy-start.3 = (s32[128]{0:T(128)S(1)}, s32[128]{0:T(128)}, u32[]{:S(2)}) copy-start(s32[128]{0:T(128)} %param.14) | copy-start | bytes 1540
  87.8 18.6 %all-to-all-start.1 = ((bf16[16,2,8192]{2,1,0:T(2,128)(2,1)}), bf16[16,2,8192]{2,1,0:T(2,128)(2,1)S(1)}, u32[]{:S(2)}, u32[]{:S(2)}) async-start(bf16[16,2,8192]{2,1,0:T(2,128)(2,1)} %reshape.473), calls=%async_computation.1 | async-start | bytes 1048576 | tf_op jit(solution)/shard_map/all_to_all | solution.py:103
  92.4 106.7 %copy-start.1 = (s32[128]{0:T(128)S(1)}, s32[128]{0:T(128)}, u32[]{:S(2)}) copy-start(s32[128]{0:T(128)} %param.15) | copy-start | bytes 1540
  106.4 23.8 %all-to-all-start = ((bf16[16,2,8192]{2,1,0:T(2,128)(2,1)}), bf16[16,2,8192]{2,1,0:T(2,128)(2,1)S(1)}, u32[]{:S(2)}, u32[]{:S(2)}) async-start(bf16[16,2,8192]{2,1,0:T(2,128)(2,1)} %reshape.471), calls=%async_computation | async-start | bytes 1048576 | tf_op jit(solution)/shard_map/all_to_all | solution.py:102
Sparse Core Ops, SparseCore 0:
  84.0 113.3 reduce-scatter.1
where the time goes:
time: 207 us; the launch traced here: 206 us
  waiting for transfers between devices  108 us (52%)
  local copies, waits for them, and re-layouts  27.2 us (13%)
  matrix products  26.4 us (13%)
  starting transfers between devices  19.9 us (10%)
  between operations  14.5 us (7%)
  other arithmetic  9.6 us (5%)
    reduce_scatter x1, waiting for transfers between devices, body(): lax.psum_scatter(lax.dot_general(out_weight, mixed, (((0,), (1,)), ((), (...  64.4 us
    dot_general x1, matrix products, body(): lax.dot_general(out_weight, mixed, (((0,), (1,)), ((), ())), preferred_el...  18.6 us
    all_to_all x1, waiting for transfers between devices, body(): lax.all_to_all(outgoing_keys, 'ctx', split_axis=0, concat_axis=0, tiled=T...  16.3 us
    unnamed x28, local copies, waits for them, and re-layouts  12.3 us
    all_to_all x1, waiting for transfers between devices, body(): lax.all_to_all(outgoing_values, 'ctx', split_axis=0, concat_axis=0, tiled...  11.5 us
    all_to_all x1, waiting for transfers between devices, body(): lax.all_to_all(keys_by_head[target], 'ctx', split_axis=0, concat_axis=0,...  9.09 us
    all_to_all x1, starting transfers between devices, body(): lax.all_to_all(keys_by_head[target], 'ctx', split_axis=0, concat_axis=0,...  7.39 us
    all_to_all x1, waiting for transfers between devices, body(): lax.all_to_all(values_by_head[target], 'ctx', split_axis=0, concat_axis=0...  7.03 us
  transfers between devices with their start and end apart: 5, of which 5 were waited for; matrix products, arithmetic and copies ran while one was open for 11% of the time, Pallas kernels for 0%

commit v1 on v0

--- a/solution.py
+++ b/solution.py
@@ -1,8 +1,11 @@
+import functools
 import math
 
 import jax
 import jax.numpy as jnp
 from jax import lax
+from jax.experimental import pallas as pl
+from jax.experimental.pallas import tpu as pltpu
 from jax.sharding import PartitionSpec as P
 
 H = 128
@@ -104,8 +107,15 @@
     )
     assembled_pages = here_index * slot_count + jnp.arange(slot_count, dtype=jnp.int32)
     sender = page_source[assembled_pages] // slot_count
-    new_keys = arrived_keys[sender].reshape(slot_count * PAGE, KV * HD)
-    new_values = arrived_values[sender].reshape(slot_count * PAGE, KV * HD)
+    picking = (sender[:, None] == jnp.arange(devices, dtype=jnp.int32)[None, :]).astype(
+        jnp.bfloat16
+    )
+    new_keys = jnp.dot(picking, arrived_keys, preferred_element_type=jnp.float32).astype(
+        jnp.bfloat16
+    ).reshape(slot_count * PAGE, KV * HD)
+    new_values = jnp.dot(picking, arrived_values, preferred_element_type=jnp.float32).astype(
+        jnp.bfloat16
+    ).reshape(slot_count * PAGE, KV * HD)
     local_keys = slot_keys.reshape(slot_count * PAGE, KV * HD)
     local_values = slot_values.reshape(slot_count * PAGE, KV * HD)
     local_tokens = local_keys.shape[0]
@@ -113,12 +123,11 @@
         queries.astype(jnp.float32).reshape(query_count, local_heads, HD), query_positions
     )
     own_queries = turned_q.astype(jnp.bfloat16).transpose(1, 0, 2)
-    target = jnp.arange(devices, dtype=jnp.int32) * local_heads // per_group
     keys_by_head = local_keys.reshape(local_tokens, KV, HD).transpose(1, 0, 2)
     values_by_head = local_values.reshape(local_tokens, KV, HD).transpose(1, 0, 2)
     head_keys, head_values = (
-        lax.all_to_all(keys_by_head[target], "ctx", split_axis=0, concat_axis=0, tiled=True),
-        lax.all_to_all(values_by_head[target], "ctx", split_axis=0, concat_axis=0, tiled=True),
+        lax.all_to_all(jnp.repeat(keys_by_head, per_group // local_heads, axis=0), "ctx", split_axis=0, concat_axis=0, tiled=True),
+        lax.all_to_all(jnp.repeat(values_by_head, per_group // local_heads, axis=0), "ctx", split_axis=0, concat_axis=0, tiled=True),
     )
     key_positions = (page_offsets[inverse][:, None] + in_page[None, :]).reshape(-1)
     key_live = (in_page[None, :] < page_lengths[inverse][:, None]).reshape(-1)
@@ -175,6 +184,494 @@
     return (new_keys, new_values, output)
 
 
+def fused_kernel(
+    n,
+    source_ref,
+    length_ref,
+    offset_ref,
+    position_ref,
+    freq_ref,
+    position_row,
+    pool_keys,
+    pool_values,
+    key_scales,
+    value_scales,
+    queries,
+    weight,
+    out_keys,
+    out_values,
+    out,
+    wv,
+    kbuf,
+    vbuf,
+    scale_own,
+    scale_all,
+    scale_rows,
+    cos_page,
+    sin_page,
+    cos_query,
+    sin_query,
+    turned,
+    keys,
+    values,
+    values_t,
+    bias,
+    scores,
+    attended,
+    core_send,
+    core_recv,
+    kept,
+    y_send,
+    y_recv,
+    z_send,
+    z_recv,
+    w_sem,
+    own_sem,
+    a_send,
+    a_recv,
+    f_send,
+    f_recv,
+    p_own,
+    p_send,
+    p_recv,
+    c_ssem,
+    c_rsem,
+    y_ssem,
+    y_rsem,
+    z_ssem,
+    z_rsem,
+):
+    f32, bf16 = jnp.float32, jnp.bfloat16
+    chips = n // 2
+    planes = chips // 2
+    me = lax.axis_index("ctx")
+    core = lax.rem(me, 2)
+    chip = me // 2
+    y = lax.rem(chip, 2)
+    z = chip // 2
+    partner = chip * 2 + 1 - core
+    tokens = pool_keys.shape[0] * PAGE
+    slots = key_scales.shape[0]
+    pages = source_ref.shape[0]
+    qn = queries.shape[0]
+    heads = queries.shape[1] // HD
+    width = out.shape[1]
+    half = HD // 2
+
+    def wait_weight(d):
+        pltpu.make_async_copy(
+            weight.at[:, pl.ds(pl.multiple_of(d * width, width), width)], wv.at[d], w_sem.at[d]
+        ).wait()
+
+    @pl.loop(0, n)
+    def _(d):
+        pltpu.make_async_copy(
+            weight.at[:, pl.ds(pl.multiple_of(d * width, width), width)], wv.at[d], w_sem.at[d]
+        ).start()
+
+    scale_own[...] = jnp.zeros_like(scale_own)
+    scale_own[0, :, 0:KV] = key_scales[...]
+    scale_own[1, :, 0:KV] = value_scales[...]
+
+    def remote(src, dst, ssem, rsem, to):
+        return pltpu.make_async_remote_copy(
+            src_ref=src, dst_ref=dst, send_sem=ssem, recv_sem=rsem, device_id={"ctx": to}
+        )
+
+    barrier = pltpu.get_barrier_semaphore()
+
+    @pl.loop(1, chips)
+    def _(s):
+        pl.semaphore_signal(
+            barrier, inc=1, device_id={"ctx": lax.rem(chip + s, chips) * 2 + core}
+        )
+
+    pl.semaphore_signal(barrier, inc=1, device_id={"ctx": partner})
+    pl.semaphore_wait(barrier, chips)
+
+    def rows_of(ref, device):
+        return ref.at[pl.ds(pl.multiple_of(device * tokens, tokens), tokens), :]
+
+    def head_of(ref, head):
+        return ref.at[:, pl.ds(pl.multiple_of(head * HD, HD), HD)]
+
+    def pool_head(ref, head):
+        return ref.at[:, :, pl.ds(pl.multiple_of(head * HD, HD), HD)]
+
+    def pages_of(ref, device):
+        return ref.at[pl.ds(device * slots, slots)]
+
+    def first_hop(s):
+        to = lax.rem(chip + s, chips)
+        dev = to * 2 + core
+        return (
+            remote(pool_head(pool_keys, to), pages_of(kbuf, me), a_send.at[0, to], a_recv.at[0, chip], dev),
+            remote(pool_head(pool_values, to), pages_of(vbuf, me), a_send.at[1, to], a_recv.at[1, chip], dev),
+            remote(scale_own, scale_all.at[:, me], a_send.at[2, to], a_recv.at[2, chip], dev),
+        )
+
+    def arrivals(s):
+        frm = lax.rem(chip + s, chips)
+        dev = frm * 2 + core
+        return (
+            remote(pages_of(kbuf, dev), pages_of(kbuf, dev), a_send.at[0, frm], a_recv.at[0, frm], dev),
+            remote(pages_of(vbuf, dev), pages_of(vbuf, dev), a_send.at[1, frm], a_recv.at[1, frm], dev),
+            remote(scale_own, scale_all.at[:, dev], a_send.at[2, frm], a_recv.at[2, frm], dev),
+        )
+
+    def forward(frm, block_core):
+        dev = frm * 2 + block_core
+        return (
+            remote(pages_of(kbuf, dev), pages_of(kbuf, dev), f_send.at[0, frm], f_recv.at[0, frm], partner),
+            remote(pages_of(vbuf, dev), pages_of(vbuf, dev), f_send.at[1, frm], f_recv.at[1, frm], partner),
+            remote(scale_all.at[:, dev], scale_all.at[:, dev], f_send.at[2, frm], f_recv.at[2, frm], partner),
+        )
+
+    @pl.loop(1, chips)
+    def _(s):
+        for copy in first_hop(s):
+            copy.start()
+
+    own = (
+        pltpu.make_async_copy(pool_head(pool_keys, chip), pages_of(kbuf, me), own_sem.at[0]),
+        pltpu.make_async_copy(pool_head(pool_values, chip), pages_of(vbuf, me), own_sem.at[1]),
+        pltpu.make_async_copy(scale_own, scale_all.at[:, me], own_sem.at[2]),
+    )
+    for copy in own:
+        copy.start()
+
+    freq = freq_ref[...]
+
+    @pl.loop(0, pages, unroll=8)
+    def _(c):
+        cos_page[pl.ds(c, 1), :] = freq * offset_ref[c].astype(f32)
+
+    @pl.loop(0, qn, unroll=8)
+    def _(c):
+        cos_query[pl.ds(c, 1), :] = freq * position_ref[c].astype(f32)
+
+    def angles(cos_ref, sin_ref):
+        angle = cos_ref[...]
+        lane = lax.broadcasted_iota(jnp.int32, angle.shape, 1)
+        sine = jnp.sin(angle)
+        sin_ref[...] = jnp.where(lane < half, -sine, sine)
+        cos_ref[...] = jnp.cos(angle)
+
+    for copy in own:
+        copy.wait()
+    for copy in forward(chip, core):
+        copy.start()
+    angles(cos_page, sin_page)
+    angles(cos_query, sin_query)
+
+    cosine, sine = cos_query[...], sin_query[...]
+    for h in range(heads):
+        x = queries[:, h * HD : (h + 1) * HD].astype(f32)
+        turned[h * qn : (h + 1) * qn, :] = (x * cosine + pltpu.roll(x, half, 1) * sine).astype(bf16)
+
+    @pl.loop(1, chips)
+    def _(s):
+        frm = lax.rem(chip + s, chips)
+        for copy, onward in zip(arrivals(s), forward(frm, core)):
+            copy.wait_recv()
+            onward.start()
+
+    @pl.loop(0, chips)
+    def _(frm):
+        for copy in forward(frm, 1 - core):
+            copy.wait_recv()
+
+    head_lane = lax.broadcasted_iota(jnp.int32, (n * slots, HD), 1) == chip
+    for kind in range(2):
+        block = scale_all[kind].reshape(n * slots, HD)
+        picked = jnp.sum(jnp.where(head_lane, block, 0.0), axis=1, keepdims=True)
+        scale_rows[kind] = jnp.broadcast_to(picked, (n * slots, HD))
+
+    row = lax.broadcasted_iota(jnp.int32, (PAGE, HD), 0)
+    q_row = position_row[...]
+
+    @pl.loop(0, pages, unroll=4)
+    def _(c):
+        s = source_ref[c]
+        live = row < length_ref[c]
+        where_to = pl.ds(pl.multiple_of(c * PAGE, PAGE), PAGE)
+        k = kbuf[s].astype(f32) * scale_rows[0, pl.ds(s, 1), :]
+        k = k * cos_page[pl.ds(c, 1), :] + pltpu.roll(k, half, 1) * sin_page[pl.ds(c, 1), :]
+        keys[where_to, :] = jnp.where(live, k, 0.0).astype(bf16)
+        v = vbuf[s].astype(f32) * scale_rows[1, pl.ds(s, 1), :]
+        values[where_to, :] = jnp.where(live, v, 0.0).astype(bf16)
+        allowed = jnp.logical_and(live, row + offset_ref[c] <= q_row)
+        bias[where_to, :] = jnp.where(allowed, 0.0, masked_score)
+
+    def pages_out(s):
+        to = lax.rem(chip + s, chips)
+        dev = to * 2 + core
+        return (
+            remote(rows_of(keys, dev), head_of(out_keys, chip), p_send.at[0, to], p_recv.at[0, chip], dev),
+            remote(rows_of(values, dev), head_of(out_values, chip), p_send.at[1, to], p_recv.at[1, chip], dev),
+        )
+
+    def pages_in(s):
+        frm = lax.rem(chip + s, chips)
+        dev = frm * 2 + core
+        return (
+            remote(rows_of(keys, me), head_of(out_keys, frm), p_send.at[0, frm], p_recv.at[0, frm], dev),
+            remote(rows_of(values, me), head_of(out_values, frm), p_send.at[1, frm], p_recv.at[1, frm], dev),
+        )
+
+    @pl.loop(1, chips)
+    def _(s):
+        for copy in pages_out(s):
+            copy.start()
+
+    own_pages = (
+        pltpu.make_async_copy(rows_of(keys, me), head_of(out_keys, chip), p_own.at[0]),
+        pltpu.make_async_copy(rows_of(values, me), head_of(out_values, chip), p_own.at[1]),
+    )
+    for copy in own_pages:
+        copy.start()
+
+    total = keys.shape[0]
+    block = 256
+    for at in range(0, total, block):
+        values_t[:, at : at + block] = values[at : at + block, :].astype(f32).T.astype(bf16)
+    span = 2 * qn
+    scale = HD ** (-0.5)
+
+    @pl.loop(0, heads // 2)
+    def _(pair):
+        q2 = turned[pl.ds(pl.multiple_of(pair * span, span), span), :]
+
+        def score_block(b, peak):
+            at = pl.ds(pl.multiple_of(b * block, block), block)
+            s = lax.dot_general(
+                keys[at, :], q2, (((1,), (1,)), ((), ())), preferred_element_type=f32
+            )
+            mask = bias[at, :]
+            s = s * scale + jnp.concatenate([mask, mask], axis=1)
+            scores[at, :] = s
+            return jnp.maximum(peak, jnp.max(s, axis=0, keepdims=True))
+
+        peak = lax.fori_loop(
+            0, total // block, score_block, jnp.full((1, span), masked_score, f32), unroll=2
+        )
+
+        def weigh(b, carry):
+            denominator, summed = carry
+            start = pl.multiple_of(b * block, block)
+            p = jnp.exp(scores[pl.ds(start, block), :] - peak)
+            denominator = denominator + jnp.sum(p, axis=0, keepdims=True)
+            summed = summed + jnp.dot(
+                values_t[:, pl.ds(start, block)], p.astype(bf16), preferred_element_type=f32
+            )
+            return denominator, summed
+
+        denominator, summed = lax.fori_loop(
+            0,
+            total // block,
+            weigh,
+            (jnp.zeros((1, span), f32), jnp.zeros((HD, span), f32)),
+            unroll=2,
+        )
+        mixed = summed / denominator
+        for j in range(2):
+            attended[:, pl.ds(pl.multiple_of((2 * pair + j) * HD, HD), HD)] = (
+                mixed[:, j * qn : (j + 1) * qn].T.astype(bf16)
+            )
+
+    piece = min(width, 256)
+
+    def project(d, store):
+        wait_weight(d)
+
+        @pl.loop(0, width, step=piece)
+        def _(at):
+            cols = pl.ds(pl.multiple_of(at, piece), piece)
+            store(
+                cols,
+                jnp.dot(attended[...], wv[d, :, cols], preferred_element_type=f32),
+            )
+
+    def across_core(t):
+        return remote(core_send.at[t], core_recv.at[t], c_ssem.at[t], c_rsem.at[t], partner)
+
+    def across_y(s):
+        dev = (z * 2 + 1 - y) * 2 + core
+        return remote(y_send.at[s], y_recv.at[s], y_ssem.at[s], y_rsem.at[s], dev)
+
+    def across_z(s):
+        dev = (lax.rem(z + 1 + s, planes) * 2 + y) * 2 + core
+        return remote(z_send.at[s], z_recv.at[s], z_ssem.at[s], z_rsem.at[s], dev)
+
+    def chip_sum(s, other):
+        t = 2 * s + (0 if other else 1)
+        q = lax.rem(z + 1 + s, planes) * 2 + (1 - y if other else y)
+
+        def to_partner(cols, x):
+            core_send[t, :, cols] = x.astype(bf16)
+
+        project(q * 2 + 1 - core, to_partner)
+        across_core(t).start()
+
+        def keep(cols, x):
+            kept[s, :, cols] = x
+
+        project(q * 2 + core, keep)
+        across_core(t).wait_recv()
+
+    @pl.loop(0, planes)
+    def _(s):
+        chip_sum(s, True)
+        y_send[s] = (kept[s] + core_recv[2 * s].astype(f32)).astype(bf16)
+        across_y(s).start()
+
+    @pl.loop(0, planes)
+    def _(s):
+        chip_sum(s, False)
+        kept[s] = kept[s] + core_recv[2 * s + 1].astype(f32)
+
+    @pl.loop(0, planes - 1)
+    def _(s):
+        across_y(s).wait_recv()
+        z_send[s] = (kept[s] + y_recv[s].astype(f32)).astype(bf16)
+        across_z(s).start()
+
+    across_y(planes - 1).wait_recv()
+    kept[planes - 1] = kept[planes - 1] + y_recv[planes - 1].astype(f32)
+
+    @pl.loop(0, planes - 1)
+    def _(s):
+        across_z(s).wait_recv()
+        kept[planes - 1] = kept[planes - 1] + z_recv[s].astype(f32)
+
+    out[...] = kept[planes - 1].astype(bf16)
+
+    for copy in own_pages:
+        copy.wait()
+
+    @pl.loop(1, chips)
+    def _(s):
+        for copy in pages_in(s):
+            copy.wait_recv()
+        for copy in pages_out(s):
+            copy.wait_send()
+        for copy in first_hop(s):
+            copy.wait_send()
+
+    @pl.loop(0, chips)
+    def _(frm):
+        for copy in forward(frm, core):
+            copy.wait_send()
+
+    @pl.loop(0, planes)
+    def _(s):
+        across_core(2 * s).wait_send()
+        across_core(2 * s + 1).wait_send()
+        across_y(s).wait_send()
+
+    @pl.loop(0, planes - 1)
+    def _(s):
+        across_z(s).wait_send()
+
+
+def fused_body(
+    pool_keys,
+    pool_values,
+    key_scales,
+    value_scales,
+    page_source,
+    page_lengths,
+    page_offsets,
+    query_positions,
+    queries,
+    out_weight,
+):
+    n = lax.axis_size("ctx")
+    chips = n // 2
+    planes = chips // 2
+    tokens, features = pool_keys.shape
+    total = n * tokens
+    slots = key_scales.shape[0]
+    pages = page_source.shape[0]
+    qn = queries.shape[0]
+    heads = queries.shape[1] // HD
+    rows, columns = out_weight.shape
+    width = columns // n
+    f32, bf16 = jnp.float32, jnp.bfloat16
+    freq = jnp.tile(inverse_freq()[None, :], (1, 2))
+    smem = pl.BlockSpec(memory_space=pltpu.SMEM)
+    vmem = pl.BlockSpec(memory_space=pltpu.VMEM)
+    hbm = pl.BlockSpec(memory_space=pl.ANY)
+    dma = pltpu.SemaphoreType.DMA
+    return pl.pallas_call(
+        functools.partial(fused_kernel, n),
+        out_shape=(
+            jax.ShapeDtypeStruct((tokens, features), bf16),
+            jax.ShapeDtypeStruct((tokens, features), bf16),
+            jax.ShapeDtypeStruct((qn, width), bf16),
+        ),
+        in_specs=[smem] * 4 + [vmem, vmem, hbm, hbm, vmem, vmem, vmem, hbm],
+        out_specs=(hbm, hbm, vmem),
+        scratch_shapes=[
+            pltpu.VMEM((n, rows, width), bf16),
+            pltpu.VMEM((pages, PAGE, HD), bf16),
+            pltpu.VMEM((pages, PAGE, HD), bf16),
+            pltpu.VMEM((2, slots, HD), f32),
+            pltpu.VMEM((2, n, slots, HD), f32),
+            pltpu.VMEM((2, n * slots, HD), f32),
+            pltpu.VMEM((pages, HD), f32),
+            pltpu.VMEM((pages, HD), f32),
+            pltpu.VMEM((qn, HD), f32),
+            pltpu.VMEM((qn, HD), f32),
+            pltpu.VMEM((heads * qn, HD), bf16),
+            pltpu.VMEM((total, HD), bf16),
+            pltpu.VMEM((total, HD), bf16),
+            pltpu.VMEM((HD, total), bf16),
+            pltpu.VMEM((total, qn), f32),
+            pltpu.VMEM((total, 2 * qn), f32),
+            pltpu.VMEM((qn, heads * HD), bf16),
+            pltpu.VMEM((chips, qn, width), bf16),
+            pltpu.VMEM((chips, qn, width), bf16),
+            pltpu.VMEM((planes, qn, width), f32),
+            pltpu.VMEM((planes, qn, width), bf16),
+            pltpu.VMEM((planes, qn, width), bf16),
+            pltpu.VMEM((planes - 1, qn, width), bf16),
+            pltpu.VMEM((planes - 1, qn, width), bf16),
+            dma((n,)),
+            dma((3,)),
+            dma((3, chips)),
+            dma((3, chips)),
+            dma((3, chips)),
+            dma((3, chips)),
+            dma((2,)),
+            dma((2, chips)),
+            dma((2, chips)),
+            dma((chips,)),
+            dma((chips,)),
+            dma((planes,)),
+            dma((planes,)),
+            dma((planes - 1,)),
+            dma((planes - 1,)),
+        ],
+        compiler_params=pltpu.CompilerParams(
+            collective_id=0, has_side_effects=True, vmem_limit_bytes=60 * 2**20
+        ),
+    )(
+        page_source,
+        page_lengths,
+        page_offsets,
+        query_positions,
+        freq,
+        query_positions.reshape(1, qn),
+        pool_keys.reshape(slots, PAGE, features),
+        pool_values.reshape(slots, PAGE, features),
+        key_scales,
+        value_scales,
+        queries,
+        out_weight,
+    )
+
+
 def solution(mesh):
     in_specs = (
         P(("groups", "ctx"), None),
@@ -189,4 +686,5 @@
         P("ctx", None),
     )
     out_specs = (P(("groups", "ctx"), None), P(("groups", "ctx"), None), P("groups", "ctx"))
-    return jax.shard_map(body, mesh=mesh, in_specs=in_specs, out_specs=out_specs, check_vma=False)
+    chosen = fused_body if mesh.shape["ctx"] == 2 * KV else body
+    return jax.shard_map(chosen, mesh=mesh, in_specs=in_specs, out_specs=out_specs, check_vma=False)

time: 207 us -> 83.8 us (0.40)
  the two profiles are of different devices: /device:TPU:0 before, /device:TPU:29 now
where the time goes in v1:
time: 83.8 us; the launch traced here: 83.6 us
  Pallas kernels  77.3 us (92%)
  local copies, waits for them, and re-layouts  5.6 us (7%)
    pallas_call x1, Pallas kernels, fused_body(): pl.pallas_call(functools.partial(fused_kernel, n), out_shape=(jax.ShapeDt...  77.3 us
    unnamed x3, local copies, waits for them, and re-layouts  5.01 us

profile of v1, /device:TPU:29, one launch (start us, length us, event | category | flops | bytes accessed | tf_op | source)
XLA Modules:
  0.0 83.6 jit_solution(13334577688067402465)
XLA Ops:
  0.7 0.6 tile.9.freq_ref
  1.3 77.3 %shard_map.121 = (bf16[128,1024]{1,0:T(8,128)(2,1)}, bf16[128,1024]{1,0:T(8,128)(2,1)}, bf16[128,1024]{1,0:T(8,128)(2,1)}) custom-call(s32[128]{0:T(128)} %source_ref.1, s32[128]{0:T(128)} %length_ref.1, s32[128]{0:T(128)} %offset_ref.1, s32[128]{0:T(128)} %position_ref.1, f32[1,128]{1,0:T(1,128)} %tile.9.freq_ref, s32[1,128]{1,0:T(1,128)} %bitcast.5, ...), custom_call_target="tpu_custom_call" | custom-call | tf_op jit(solution)/shard_map/pallas_call | solution.py:606
  78.6 1.7 %copy.16 = bf16[128,1024]{1,0:T(8,128)(2,1)} copy(bf16[128,1024]{1,0:T(8,128)(2,1)} %get-tuple-element.6) | data formatting | bytes 524288
  80.3 1.7 %copy.17 = bf16[128,1024]{1,0:T(8,128)(2,1)} copy(bf16[128,1024]{1,0:T(8,128)(2,1)} %get-tuple-element.7) | data formatting | bytes 524288
  81.9 1.7 %copy.18 = bf16[128,1024]{1,0:T(8,128)(2,1)} copy(bf16[128,1024]{1,0:T(8,128)(2,1)} %get-tuple-element.8) | data formatting | bytes 524288
  (2 shorter events, 0.0 us)

commit v2 on v1

--- a/solution.py
+++ b/solution.py
@@ -182,6 +182,9 @@
     )
     output = reduced.T.astype(jnp.bfloat16)
     return (new_keys, new_values, output)
+
+
+PIECE = 1024
 
 
 def fused_kernel(
@@ -479,7 +482,7 @@
                 mixed[:, j * qn : (j + 1) * qn].T.astype(bf16)
             )
 
-    piece = min(width, 256)
+    piece = min(width, PIECE)
 
     def project(d, store):
         wait_weight(d)
@@ -503,32 +506,46 @@
         dev = (lax.rem(z + 1 + s, planes) * 2 + y) * 2 + core
         return remote(z_send.at[s], z_recv.at[s], z_ssem.at[s], z_rsem.at[s], dev)
 
-    def chip_sum(s, other):
-        t = 2 * s + (0 if other else 1)
-        q = lax.rem(z + 1 + s, planes) * 2 + (1 - y if other else y)
-
-        def to_partner(cols, x):
-            core_send[t, :, cols] = x.astype(bf16)
-
-        project(q * 2 + 1 - core, to_partner)
-        across_core(t).start()
-
-        def keep(cols, x):
-            kept[s, :, cols] = x
-
-        project(q * 2 + core, keep)
-        across_core(t).wait_recv()
+    def chip_at(k):
+        return lax.rem(z + 1 + lax.rem(k, planes), planes) * 2 + lax.rem(1 - y + k // planes, 2)
+
+    def for_partner(k):
+        def store(cols, x):
+            core_send[k, :, cols] = x.astype(bf16)
+
+        project(chip_at(k) * 2 + 1 - core, store)
+        across_core(k).start()
+
+    def for_neighbour(k):
+        across_core(k).wait_recv()
+
+        def store(cols, x):
+            y_send[k, :, cols] = (x + core_recv[k, :, cols].astype(f32)).astype(bf16)
+
+        project(chip_at(k) * 2 + core, store)
+        across_y(k).start()
+
+    def for_column(k):
+        across_core(k).wait_recv()
+
+        def store(cols, x):
+            kept[k - planes, :, cols] = x + core_recv[k, :, cols].astype(f32)
+
+        project(chip_at(k) * 2 + core, store)
+
+    for_partner(0)
 
     @pl.loop(0, planes)
-    def _(s):
-        chip_sum(s, True)
-        y_send[s] = (kept[s] + core_recv[2 * s].astype(f32)).astype(bf16)
-        across_y(s).start()
-
-    @pl.loop(0, planes)
-    def _(s):
-        chip_sum(s, False)
-        kept[s] = kept[s] + core_recv[2 * s + 1].astype(f32)
+    def _(k):
+        for_partner(k + 1)
+        for_neighbour(k)
+
+    @pl.loop(planes, chips - 1)
+    def _(k):
+        for_partner(k + 1)
+        for_column(k)
+
+    for_column(chips - 1)
 
     @pl.loop(0, planes - 1)
     def _(s):
@@ -565,13 +582,26 @@
 
     @pl.loop(0, planes)
     def _(s):
-        across_core(2 * s).wait_send()
-        across_core(2 * s + 1).wait_send()
+        across_core(s).wait_send()
+        across_core(s + planes).wait_send()
         across_y(s).wait_send()
 
     @pl.loop(0, planes - 1)
     def _(s):
         across_z(s).wait_send()
+
+
+def hand_over(a, b, c, a_out, b_out, c_out, a_buf, b_buf, c_buf, sem):
+    ways = ((a, a_buf, a_out), (b, b_buf, b_out), (c, c_buf, c_out))
+    inward = [pltpu.make_async_copy(s, v, sem.at[0, i]) for i, (s, v, _) in enumerate(ways)]
+    outward = [pltpu.make_async_copy(v, d, sem.at[1, i]) for i, (_, v, d) in enumerate(ways)]
+    for copy in inward:
+        copy.start()
+    for arrive, leave in zip(inward, outward):
+        arrive.wait()
+        leave.start()
+    for copy in outward:
+        copy.wait()
 
 
 def fused_body(
@@ -603,7 +633,7 @@
     vmem = pl.BlockSpec(memory_space=pltpu.VMEM)
     hbm = pl.BlockSpec(memory_space=pl.ANY)
     dma = pltpu.SemaphoreType.DMA
-    return pl.pallas_call(
+    results = pl.pallas_call(
         functools.partial(fused_kernel, n),
         out_shape=(
             jax.ShapeDtypeStruct((tokens, features), bf16),
@@ -670,6 +700,13 @@
         queries,
         out_weight,
     )
+    return pl.pallas_call(
+        hand_over,
+        out_shape=tuple(jax.ShapeDtypeStruct(r.shape, r.dtype) for r in results),
+        in_specs=[hbm] * 3,
+        out_specs=(hbm, hbm, hbm),
+        scratch_shapes=[pltpu.VMEM(r.shape, r.dtype) for r in results] + [dma((2, 3))],
+    )(*results)
 
 
 def solution(mesh):

time: 83.8 us -> 73.6 us (0.88)
  the two profiles are of different devices: /device:TPU:29 before, /device:TPU:0 now
where the time goes in v2:
time: 73.6 us; the launch traced here: 73.4 us
  Pallas kernels  72.2 us (98%)
    pallas_call x1, Pallas kernels, fused_body(): pl.pallas_call(functools.partial(fused_kernel, n), out_shape=(jax.ShapeDt...  70.3 us
    pallas_call x1, Pallas kernels, fused_body(): pl.pallas_call(hand_over, out_shape=tuple((jax.ShapeDtypeStruct(r.shape,...  1.88 us

profile of v2, /device:TPU:0, one launch (start us, length us, event | category | flops | bytes accessed | tf_op | source)
XLA Modules:
  0.0 73.4 jit_solution(13197881974173024133)
XLA Ops:
  0.7 0.6 tile.9.freq_ref
  1.3 70.3 %shard_map.121 = (bf16[128,1024]{1,0:T(8,128)(2,1)}, bf16[128,1024]{1,0:T(8,128)(2,1)}, bf16[128,1024]{1,0:T(8,128)(2,1)}) custom-call(s32[128]{0:T(128)} %source_ref.1, s32[128]{0:T(128)} %length_ref.1, s32[128]{0:T(128)} %offset_ref.1, s32[128]{0:T(128)} %position_ref.1, f32[1,128]{1,0:T(1,128)} %tile.9.freq_ref, s32[1,128]{1,0:T(1,128)} %bitcast.5, ...), custom_call_target="tpu_custom_call" | custom-call | tf_op jit(solution)/shard_map/pallas_call | solution.py:636
  71.6 1.9 %shard_map.122 = (bf16[128,1024]{1,0:T(8,128)(2,1)}, bf16[128,1024]{1,0:T(8,128)(2,1)}, bf16[128,1024]{1,0:T(8,128)(2,1)}) custom-call(bf16[128,1024]{1,0:T(8,128)(2,1)} %get-tuple-element.6.a, bf16[128,1024]{1,0:T(8,128)(2,1)} %get-tuple-element.7.b, bf16[128,1024]{1,0:T(8,128)(2,1)} %get-tuple-element.8.c), custom_call_target="tpu_custom_call" | custom-call | tf_op jit(solution)/shard_map/pallas_call | solution.py:703
  (2 shorter events, 0.0 us)
